TPU v7x, 32 devices: a whole 2x2x4 slice. The times are simulated.
32 devices in a mesh: leaf: 16 (over z, y, x), cone: 2 (over core).
Axes of the slice: x: 2, y: 2, z: 4, core: 2. Of those that a mesh axis runs over, the one named last changes fastest.
Arguments:
- coefficients: bfloat16 [128, 4, 3, 32, 256], P('leaf', 'cone'), may hold values from -6 to 6
- local_to_target: bfloat16 [128, 4, 256, 768], P('leaf', 'cone'), may hold values from -0.1875 to 0.1875
- send_map: int32 [16, 16, 32], P('leaf'), may hold values from -1 to 255, as said below
- test_weight: bfloat16 [16, 16, 32, 108], P('leaf'), may hold values from -1 to 1
- slot_edge: int32 [3, 16, 16, 32], P(None, 'leaf'), may hold values from -1 to 383, as said below
- shared_edges: int32 [16, 2, 32], P('leaf'), may hold values from 0 to 383, as said below
Outputs:
- tested: float32 [2, 32, 6144], P(None, 'cone', 'leaf')
Inputs may be any that keep to these rules, and one draw needn't show every extreme that they name: Each of the 256 triangles of a leaf device s stands in exactly one slot of send_map[s]; every other slot is -1. In every draw, each leaf device fills all 32 slots of its block to some owner. slot_edge[e, d, s, n] is -1 exactly where send_map[s, d, n] is -1. The 64 numbers of shared_edges[d] are distinct.
All inputs are finite; a program needn't handle non-finite values.
Results may differ from a plain program's by a relative error of at most 0.0029.
Values may be sent and summed in bfloat16 or wider, within the bound.
A program may use at most 64 MiB of HBM per device.

v0:
```python
import jax
import jax.numpy as jnp
from jax import lax
from jax.sharding import PartitionSpec as P

QUAD = 12
TRI_LEAF = 32
EDGE_DEV = 384


def extended(array, sides, width):
    for axis, dim in sides:
        peers, length = (lax.axis_size(axis), array.shape[dim])
        up = [(i, (i + 1) % peers) for i in range(peers - 1)]
        down = [(j, i) for i, j in up]
        last = lax.slice_in_dim(array, length - width, length, axis=dim)
        leading = lax.slice_in_dim(array, 0, width, axis=dim)
        before = lax.ppermute(last, axis, up)
        after = lax.ppermute(leading, axis, down)
        array = jnp.concatenate([before, array, after], axis=dim)
    return array


def tested_slots(weights, fields, rhs_count, result_form):
    peer_count, capacity = (weights.shape[0], weights.shape[1])
    weight_view = weights.reshape(peer_count, capacity, 3, QUAD, 3)
    field_view = fields.reshape(peer_count, capacity, QUAD, 2, 3, rhs_count)
    return jnp.einsum(
        "scepk,scpikh->" + result_form, weight_view, field_view, preferred_element_type=jnp.float32
    )


def body(coefficients, local_to_target, send_map, test_weight, slot_edge, shared_edges):
    partial_field = jnp.einsum(
        "lkchr,lkrq->lqch", coefficients, local_to_target, preferred_element_type=jnp.float32
    )
    cone_count = lax.axis_size("cone")
    rhs_count = partial_field.shape[3] // cone_count
    summed = lax.psum(partial_field, "cone")
    rhs_share = lax.dynamic_slice_in_dim(summed, lax.axis_index("cone") * rhs_count, rhs_count, 3)
    rhs_share = rhs_share.astype(jnp.bfloat16)
    leaf_count = rhs_share.shape[0]
    tri_rows = rhs_share.reshape(leaf_count * TRI_LEAF, -1)
    send_rows = send_map[0]
    is_live = send_rows >= 0
    safe_rows = jnp.where(is_live, send_rows, 0)
    picked = tri_rows[safe_rows]
    outgoing = jnp.where(is_live[:, :, None], picked, jnp.zeros((), jnp.bfloat16))
    weights = test_weight[0]
    arrived = lax.all_to_all(outgoing, "leaf", split_axis=0, concat_axis=0, tiled=True)
    partial_value = tested_slots(weights, arrived, rhs_count, "escih")
    edge_ids = slot_edge[:, 0].reshape(-1)
    values = partial_value.reshape(-1, 2 * rhs_count)
    onehot = (edge_ids[:, None] == jnp.arange(EDGE_DEV, dtype=jnp.int32)[None, :]).astype(
        jnp.float32
    )
    edge_sum = jnp.einsum(
        "ra,re->ae",
        values,
        onehot,
        precision=lax.Precision.HIGHEST,
        preferred_element_type=jnp.float32,
    )
    lower_ids = shared_edges[0, 0]
    upper_ids = shared_edges[0, 1]
    share_width = lower_ids.shape[0]
    rim_values = jnp.concatenate([edge_sum[:, lower_ids], edge_sum[:, upper_ids]], axis=1)
    padded = extended(rim_values, (("leaf", 1),), share_width)
    total = (
        edge_sum.at[:, lower_ids]
        .add(padded[:, :share_width])
        .at[:, upper_ids]
        .add(padded[:, 3 * share_width :])
    )
    return total.reshape(2, rhs_count, -1)


def solution(mesh):
    placed = (
        P("leaf", "cone", None, None, None),
        P("leaf", "cone", None, None),
        P("leaf", None, None),
        P("leaf", None, None, None),
        P(None, "leaf", None, None),
        P("leaf", None, None),
    )
    return jax.shard_map(
        body, mesh=mesh, in_specs=placed, out_specs=P(None, "cone", "leaf"), check_vma=False
    )
```

profile of v0, /device:TPU:6, one launch (start us, length us, event | category | flops | bytes accessed | tf_op | source)
XLA Modules:
  0.0 120.5 jit_solution(16568541062340450514)
XLA Ops:
  0.0 0.0 copy-start
  0.0 0.8 compare_select_fusion
  0.8 0.7 compare_bitcast_fusion
  1.5 0.0 copy-done
  1.5 5.3 %fusion.3 = f32[8,768,3,32]{1,3,2,0:T(8,128)} fusion(bf16[8,2,3,32,256]{4,3,2,1,0:T(8,128)(2,1)S(1)} %copy-done, bf16[8,2,256,768]{3,2,1,0:T(8,128)(2,1)} %param.7), kind=kOutput, calls=%fused_computation.9 | convolution fusion | flops 603979776 | bytes 9437184 | tf_op jit(solution)/shard_map/lkchr,lkrq->lqch/dot_general | solution.py:34
  6.8 10.3 %all-reduce.1 = bf16[8,768,3,32]{1,3,2,0:T(8,128)(2,1)S(1)} all-reduce(f32[8,768,3,32]{1,3,2,0:T(8,128)} %fusion.3), channel_id=1, replica_groups=mesh['leaf'=16,'cone'=2] {'cone'}, use_global_device_ids=true, to_apply=%region_0.0 | all-reduce | flops 589824 | bytes 3538944 | tf_op jit(solution)/shard_map/psum | solution.py:39
  17.1 6.7 %copy.25 = bf16[8,768,3,16]{3,2,1,0:T(4,128)(2,1)} copy(bf16[8,768,3,16]{1,3,2,0:T(8,128)(2,1)S(1)} %dynamic-slice_convert_fusion) | data formatting | bytes 1179648 | tf_op jit(solution)/shard_map/convert_element_type | solution.py:41
  23.9 9.3 %reshape.102 = bf16[256,1152]{1,0:T(8,128)(2,1)S(1)} reshape(bf16[8,768,3,16]{3,2,1,0:T(4,128)(2,1)} %copy.25) | data formatting | bytes 1179648 | tf_op jit(solution)/shard_map/reshape | solution.py:43
  33.2 0.1 reshape.108
  33.3 2.1 %gather_fusion = bf16[512,1152]{1,0:T(8,128)(2,1)S(1)} fusion(bf16[256,1152]{1,0:T(8,128)(2,1)S(1)} %reshape.102, s32[1024]{0:T(1024)S(1)} %pad_clamp_fusion.2), kind=kCustom, calls=%fused_computation | custom fusion | bytes 2361344 | tf_op jit(solution)/shard_map/gather | solution.py:47
  35.4 0.0 copy-start.2
  35.4 1.2 %broadcast_select_fusion = bf16[16,32,1152]{2,1,0:T(8,128)(2,1)} fusion(bf16[16,32,1152]{2,1,0:T(8,128)(2,1)S(1)} %bitcast.58, pred[16,32]{1,0:T(8,128)(4,1)S(1)} %compare_bitcast_fusion), kind=kLoop, calls=%fused_computation.13 | loop fusion | flops 589824 | bytes 2359808 | tf_op jit(solution)/shard_map/jit(_where)/select_n | solution.py:48
  36.6 0.0 copy-start.3
  36.6 0.0 copy-start.4
  36.6 7.4 %all-to-all-start = ((bf16[16,32,1152]{2,1,0:T(8,128)(2,1)}), bf16[16,32,1152]{2,1,0:T(8,128)(2,1)S(1)}, u32[]{:S(2)}, u32[]{:S(2)}) async-start(bf16[16,32,1152]{2,1,0:T(8,128)(2,1)} %broadcast_select_fusion), calls=%async_computation | async-start | bytes 2359296 | tf_op jit(solution)/shard_map/all_to_all | solution.py:50
  44.0 0.0 copy-done.2
  44.0 0.4 copy.27
  44.4 2.5 %copy.37 = bf16[16,32,3,12,3,1]{3,2,4,5,1,0:T(4,128)(2,1)} copy(bf16[16,32,3,12,3,1]{1,0,4,3,2,5:T(8,128)(2,1)S(1)} %bitcast.59) | data formatting | bytes 221184 | tf_op jit(solution)/shard_map/reshape;squeeze | solution.py:26
  47.0 0.0 copy-done.3
  47.0 0.1 eq.15
  47.1 0.0 copy-done.4
  47.1 23.8 %all-to-all-done = bf16[16,32,1152]{2,1,0:T(8,128)(2,1)S(1)} async-done(((bf16[16,32,1152]{2,1,0:T(8,128)(2,1)}), bf16[16,32,1152]{2,1,0:T(8,128)(2,1)S(1)}, u32[]{:S(2)}, u32[]{:S(2)}) %all-to-all-start) | async-done | bytes 1179680 | tf_op jit(solution)/shard_map/all_to_all | solution.py:50
  70.9 3.3 %copy.26 = bf16[16,32,1152]{1,2,0:T(8,128)(2,1)} copy(bf16[16,32,1152]{2,1,0:T(8,128)(2,1)S(1)} %all-to-all-done) | data formatting | bytes 2359296 | tf_op jit(solution)/shard_map/all_to_all | solution.py:50
  74.2 0.0 copy-start.1
  74.2 19.7 %copy.28 = bf16[16,32,12,2,3,16]{5,2,4,3,1,0:T(8,128)(2,1)} copy(bf16[16,32,12,2,3,16]{1,5,4,3,2,0:T(8,128)(2,1)} %bitcast.57) | data formatting | bytes 2359296 | tf_op jit(solution)/shard_map/reshape | solution.py:27
  93.9 0.0 copy-done.1
  93.9 6.6 %convolution_bitcast_fusion = f32[3,16,32,2,16]{4,0,3,2,1:T(4,128)} fusion(bf16[16,32,12,2,3,16]{5,2,4,3,1,0:T(8,128)(2,1)} %copy.28, bf16[16,32,3,12,3,1]{3,2,4,5,1,0:T(4,128)(2,1)S(1)} %copy-done.1), kind=kOutput, calls=%fused_computation.10 | convolution fusion | flops 3538944 | bytes 1486848 | tf_op jit(solution)/shard_map/scepk,scpikh->escih/dot_general | solution.py:28
  100.5 1.8 %copy.30 = f32[3,16,32,2,16]{2,1,0,4,3:T(8,128)S(1)} copy(f32[3,16,32,2,16]{4,0,3,2,1:T(4,128)} %convolution_bitcast_fusion) | data formatting | bytes 393216 | tf_op jit(solution)/shard_map/scepk,scpikh->escih/transpose | solution.py:28
  102.4 0.3 reshape.104
  102.7 2.2 %fusion.2 = f32[32,384]{0,1:T(8,128)S(1)} fusion(f32[1536,32]{0,1:T(8,128)S(1)} %reshape.104, s32[1536]{0:T(1024)S(1)} %eq.15), kind=kOutput, calls=%fused_computation.8 | convolution fusion | flops 227082240 | bytes 251904 | tf_op jit(solution)/shard_map/ra,re->ae/dot_general | solution.py:57
  104.9 0.6 gather_fusion.1
  105.5 5.4 %collective-permute-start = (f32[32,32]{0,1:T(8,128)S(1)}, f32[32,32]{0,1:T(8,128)S(1)}, u32[]{:S(2)}, u32[]{:S(2)}) collective-permute-start(f32[32,32]{0,1:T(8,128)S(1)} %bitcast.61), channel_id=1, source_target_pairs={{0,2},{2,4},{4,6},{6,8},{8,10},{10,12},{12,14},{14,16},{16,18},{18... | collective-permute-start | bytes 12296 | tf_op jit(solution)/shard_map/ppermute | solution.py:18
  111.0 0.6 gather_fusion.2
  111.5 1.9 %collective-permute-start.1 = (f32[32,32]{0,1:T(8,128)S(1)}, f32[32,32]{0,1:T(8,128)S(1)}, u32[]{:S(2)}, u32[]{:S(2)}) collective-permute-start(f32[32,32]{0,1:T(8,128)S(1)} %bitcast.60), channel_id=1, source_target_pairs={{2,0},{4,2},{6,4},{8,6},{10,8},{12,10},{14,12},{16,14},{18,16},{20... | collective-permute-start | bytes 12296 | tf_op jit(solution)/shard_map/ppermute | solution.py:19
  113.5 0.0 collective-permute-done
  113.5 0.8 scatter_custom_fusion
  114.3 4.6 %collective-permute-done.1 = f32[32,32]{0,1:T(8,128)S(1)} collective-permute-done((f32[32,32]{0,1:T(8,128)S(1)}, f32[32,32]{0,1:T(8,128)S(1)}, u32[]{:S(2)}, u32[]{:S(2)}) %collective-permute-start.1) | collective-permute-done | bytes 4128 | tf_op jit(solution)/shard_map/ppermute | solution.py:19
  119.0 0.8 scatter_custom_fusion.1
  119.8 0.7 copy.34
  (4 shorter events, 0.1 us)
Async XLA Ops:
  0.0 1.5 %copy-start = (bf16[8,2,3,32,256]{4,3,2,1,0:T(8,128)(2,1)S(1)}, bf16[8,2,3,32,256]{4,3,2,1,0:T(8,128)(2,1)}, u32[]{:S(2)}) copy-start(bf16[8,2,3,32,256]{4,3,2,1,0:T(8,128)(2,1)} %param.6) | copy-start | bytes 2359300
  35.4 8.6 %copy-start.2 = (bf16[1,16,32,108]{3,2,1,0:T(8,128)(2,1)S(1)}, bf16[1,16,32,108]{3,2,1,0:T(8,128)(2,1)}, u32[]{:S(2)}) copy-start(bf16[1,16,32,108]{3,2,1,0:T(8,128)(2,1)} %param.9) | copy-start | bytes 331780
  36.6 10.3 %copy-start.3 = (s32[3,1,16,32]{3,2,1,0:T(8,128)S(1)}, s32[3,1,16,32]{3,2,1,0:T(8,128)}, u32[]{:S(2)}) copy-start(s32[3,1,16,32]{3,2,1,0:T(8,128)} %param.10) | copy-start | bytes 18436
  36.6 10.4 %copy-start.4 = (s32[1,2,32]{2,1,0:T(2,128)S(1)}, s32[1,2,32]{2,1,0:T(2,128)}, u32[]{:S(2)}) copy-start(s32[1,2,32]{2,1,0:T(2,128)} %param.11) | copy-start | bytes 772
  36.6 34.2 %all-to-all-start = ((bf16[16,32,1152]{2,1,0:T(8,128)(2,1)}), bf16[16,32,1152]{2,1,0:T(8,128)(2,1)S(1)}, u32[]{:S(2)}, u32[]{:S(2)}) async-start(bf16[16,32,1152]{2,1,0:T(8,128)(2,1)} %broadcast_select_fusion), calls=%async_computation | async-start | bytes 2359296 | tf_op jit(solution)/shard_map/all_to_all | solution.py:50
  74.2 19.7 %copy-start.1 = (bf16[16,32,3,12,3,1]{3,2,4,5,1,0:T(4,128)(2,1)S(1)}, bf16[16,32,3,12,3,1]{3,2,4,5,1,0:T(4,128)(2,1)}, u32[]{:S(2)}) copy-start(bf16[16,32,3,12,3,1]{3,2,4,5,1,0:T(4,128)(2,1)} %copy.37) | copy-start | bytes 331780
  105.5 7.9 %collective-permute-start = (f32[32,32]{0,1:T(8,128)S(1)}, f32[32,32]{0,1:T(8,128)S(1)}, u32[]{:S(2)}, u32[]{:S(2)}) collective-permute-start(f32[32,32]{0,1:T(8,128)S(1)} %bitcast.61), channel_id=1, source_target_pairs={{0,2},{2,4},{4,6},{6,8},{8,10},{10,12},{12,14},{14,16},{16,18},{18... | collective-permute-start | bytes 12296 | tf_op jit(solution)/shard_map/ppermute | solution.py:18
  111.5 7.4 %collective-permute-start.1 = (f32[32,32]{0,1:T(8,128)S(1)}, f32[32,32]{0,1:T(8,128)S(1)}, u32[]{:S(2)}, u32[]{:S(2)}) collective-permute-start(f32[32,32]{0,1:T(8,128)S(1)} %bitcast.60), channel_id=1, source_target_pairs={{2,0},{4,2},{6,4},{8,6},{10,8},{12,10},{14,12},{16,14},{18,16},{20... | collective-permute-start | bytes 12296 | tf_op jit(solution)/shard_map/ppermute | solution.py:19
where the time goes:
time: 121 us
  local copies, waits for them, and re-layouts  48.4 us (40%)
  waiting for transfers between devices  28.4 us (23%)
  starting transfers between devices  14.7 us (12%)
  matrix products  14.2 us (12%)
  blocking collectives  10.3 us (9%)
  other arithmetic  4.39 us (4%)
    all_to_all x1, waiting for transfers between devices, body(): lax.all_to_all(outgoing, 'leaf', split_axis=0, concat_axis=0, tiled=True)  23.8 us
    reshape x1, local copies, waits for them, and re-layouts, tested_slots(): field_view = fields.reshape(peer_count, capacity, QUAD, 2, 3, rhs_count)  19.7 us
    psum x1, blocking collectives, body(): summed = lax.psum(partial_field, 'cone')  10.3 us
    reshape x1, local copies, waits for them, and re-layouts, body(): tri_rows = rhs_share.reshape(leaf_count * TRI_LEAF, -1)  9.31 us
    all_to_all x1, starting transfers between devices, body(): lax.all_to_all(outgoing, 'leaf', split_axis=0, concat_axis=0, tiled=True)  7.4 us
    convert_element_type x2, local copies, waits for them, and re-layouts, body(): rhs_share = rhs_share.astype(jnp.bfloat16)  6.78 us
    dot_general x1, matrix products, tested_slots(): jnp.einsum('scepk,scpikh->' + result_form, weight_view, field_view, prefe...  6.63 us
    ppermute x1, starting transfers between devices, extended(): before = lax.ppermute(last, axis, up)  5.42 us
  transfers between devices with their start and end apart: 3, of which 2 were waited for; matrix products, arithmetic and copies ran while one was open for 4% of the time, Pallas kernels for 0%

commit v1 on v0

v1 whole, which is shorter than its diff:
```python
import functools

import jax
import jax.numpy as jnp
from jax import lax
from jax.experimental import pallas as pl
from jax.experimental.pallas import tpu as pltpu
from jax.sharding import PartitionSpec as P

QUAD = 12
TRI_LEAF = 32
EDGE_DEV = 384
LANES = 128
GROUP = 16
MESH = pl.DeviceIdType.MESH
F32 = jnp.float32
BF16 = jnp.bfloat16
NT = (((1,), (1,)), ((), ()))


def iota(shape, dim):
    return lax.broadcasted_iota(jnp.int32, shape, dim)


def bits(mask):
    return jnp.where(mask, 1.0, 0.0).astype(BF16)


def dot(a, b):
    return jnp.dot(a, b, preferred_element_type=F32)


def split(x):
    hi = x.astype(BF16)
    lo = (x - hi.astype(F32)).astype(BF16)
    return hi, lo


def column(row):
    k = row.shape[1]
    eye = iota((k, k), 0) == iota((k, k), 1)
    return jnp.sum(jnp.where(eye, jnp.broadcast_to(row, (k, k)), 0), axis=1, keepdims=True)


def kernel(
    peers, cap, capp, leaves, rhs, share,
    coef_hbm, op_hbm, map_ref, weight_hbm, edge_ref, shared_ref,
    out_ref,
    coef, op, field, wpad, wbuf, route, collect, sel_x, col_x, p_own, p_send, p_recv,
    send, recv, rim, rim_low, rim_up,
    coef_sem, op_sem, wpad_sem, wown_sem, wsend_sem, wrecv_sem, psend_sem, precv_sem,
    send_sem, recv_sem, rim_send, rim_recv,
):
    me = lax.axis_index("leaf")
    core = lax.axis_index("cone")
    points = 2 * QUAD * TRI_LEAF
    tris = leaves * TRI_LEAF
    half = rhs // 2
    width = GROUP * LANES
    groups = peers // GROUP

    coef_copy = pltpu.make_async_copy(coef_hbm, coef, coef_sem)
    coef_copy.start()
    op_copies = []
    for l in range(leaves):
        copy = pltpu.make_async_copy(op_hbm.at[l], op.at[l], op_sem.at[l])
        copy.start()
        op_copies.append(copy)

    rim_low[...] = jnp.zeros_like(rim_low)
    rim_up[...] = jnp.zeros_like(rim_up)
    barrier = pltpu.get_barrier_semaphore()

    def greet(k, carry):
        pl.semaphore_signal(
            barrier, inc=1, device_id=(lax.rem(me + k, peers), core), device_id_type=MESH
        )
        return carry

    lax.fori_loop(1, peers, greet, 0)
    pl.semaphore_signal(barrier, inc=1, device_id=(me, 1 - core), device_id_type=MESH)

    if capp == cap:
        weight_src = weight_hbm.at[0]
    else:
        wpad[...] = jnp.zeros_like(wpad)
        rows = pltpu.make_async_copy(weight_hbm.at[0], wpad.at[:, :cap], wpad_sem)
        rows.start()
        rows.wait()
        weight_src = wpad
    own_weights = pltpu.make_async_copy(weight_src.at[me], wbuf.at[me], wown_sem)
    own_weights.start()

    pl.semaphore_wait(barrier, peers)

    def weight_copy(k):
        to = lax.rem(me + k, peers)
        return pltpu.make_async_remote_copy(
            src_ref=weight_src.at[to], dst_ref=wbuf.at[me],
            send_sem=wsend_sem.at[to], recv_sem=wrecv_sem.at[me],
            device_id=(to, core), device_id_type=MESH,
        )

    def weight_arrival(k):
        source = lax.rem(me + k, peers)
        return pltpu.make_async_remote_copy(
            src_ref=weight_src.at[source], dst_ref=wbuf.at[source],
            send_sem=wsend_sem.at[source], recv_sem=wrecv_sem.at[source],
            device_id=(source, core), device_id_type=MESH,
        )

    def start_weight(k, carry):
        weight_copy(k).start()
        return carry

    lax.fori_loop(1, peers, start_weight, 0)

    maps = map_ref[0]
    filler = jnp.full((peers, LANES - 3 * cap), -1, jnp.int32)
    sel_x[...] = jnp.concatenate([maps, maps, maps, filler], axis=1)
    col_x[...] = jnp.concatenate([edge_ref[0, 0], edge_ref[1, 0], edge_ref[2, 0], filler], axis=1)
    lower_col = column(shared_ref[0, 0:1, :])
    upper_col = column(shared_ref[0, 1:2, :])
    rim_cols = jnp.concatenate(
        [lower_col, upper_col, jnp.full((LANES - 2 * share, 1), -2, jnp.int32)], axis=0
    )
    lane_e = iota((1, LANES), 1)

    def build_route(g):
        for j in range(GROUP):
            row = sel_x[pl.ds(g * GROUP + j, 1), :]
            for e in range(3):
                ours = jnp.logical_and(lane_e >= e * cap, lane_e < (e + 1) * cap)
                key = jnp.where(ours, row, -1)
                route[e * tris:(e + 1) * tris, j * LANES:(j + 1) * LANES] = bits(
                    iota((tris, LANES), 0) == key
                )

    def build_collect(g):
        for j in range(GROUP):
            row = col_x[pl.ds(g * GROUP + j, 1), :]
            lanes = slice(j * LANES, (j + 1) * LANES)
            collect[:EDGE_DEV, lanes] = bits(iota((EDGE_DEV, LANES), 0) == row)
            collect[EDGE_DEV:, lanes] = bits(rim_cols == row)

    if groups == 1:
        build_route(0)
        build_collect(0)

    coef_copy.wait()
    for l in range(leaves):
        op_copies[l].wait()
        total = None
        for k in range(coef.shape[1]):
            term = dot(coef[l, k].reshape(3 * rhs, -1), op[l, k])
            total = term if total is None else total + term
        field[l] = total

    own_weights.wait()

    def take_weight(k, carry):
        weight_arrival(k).wait_recv()
        return carry

    lax.fori_loop(1, peers, take_weight, 0)
    if capp != cap:
        maps = jnp.concatenate([maps, jnp.full((peers, capp - cap), -1, jnp.int32)], axis=1)
    slots = jnp.concatenate([maps[d:d + 1] for d in range(peers)], axis=1)
    pick = bits(iota((tris, peers * capp), 0) == slots)
    by_tri = dot(pick, wbuf[...].reshape(peers * capp, -1)).astype(BF16)
    rows = iota((16 * QUAD, 9 * QUAD), 0)
    point, pair = rows >> 4, rows & 15
    e_of = (pair * 11) >> 5
    order = (pair < 9) & (iota(rows.shape, 1) == e_of * (3 * QUAD) + point * 3 + pair - 3 * e_of)
    turned = lax.dot_general(bits(order), by_tri, NT, preferred_element_type=F32).astype(BF16)
    tri_row = (iota((tris, points), 0) & (TRI_LEAF - 1)) * (2 * QUAD)
    lane_q = iota((tris, points), 1)
    spread = bits((lane_q >= tri_row) & (lane_q < tri_row + 2 * QUAD))
    q_row = iota((1, points), 1)
    point_of = (q_row - ((q_row * 2731) >> 16) * (2 * QUAD)) >> 1
    q_col = iota((points, 2 * LANES), 0)
    out_lane = iota((points, 2 * LANES), 1)
    first = (out_lane & (TRI_LEAF - 1)) * (2 * QUAD)
    gather = bits(
        (q_col >= first) & (q_col < first + 2 * QUAD) & ((q_col & 1) == (out_lane >> 7))
    )
    tri_lane = iota((1, tris), 1)
    lane_group = iota((1, LANES), 1) // TRI_LEAF

    per_tile = LANES // TRI_LEAF
    tiles = tris // LANES
    acc = None
    for l in range(leaves):
        mine = jnp.where((tri_lane >= l * TRI_LEAF) & (tri_lane < (l + 1) * TRI_LEAF), turned, 0)
        wide = dot(mine, spread)
        weights = None
        for p in range(QUAD):
            part = jnp.where(point_of == p, wide[p * 16:(p + 1) * 16], 0.0)
            weights = part if weights is None else weights + part
        scaled = []
        for e in range(3):
            value = None
            for c in range(3):
                term = field[l, c * rhs:(c + 1) * rhs, :] * weights[3 * e + c:3 * e + c + 1, :]
                value = term if value is None else value + term
            scaled.append(value)
        hi, lo = split(jnp.concatenate(scaled, axis=0))
        summed = dot(hi, gather) + dot(lo, gather)
        keep = jnp.where(lane_group == l % per_tile, 1.0, 0.0)
        parts = [summed[:, :LANES] * keep, summed[:, LANES:] * keep]
        acc = parts if l % per_tile == 0 else [a + b for a, b in zip(acc, parts)]
        if l % per_tile == per_tile - 1:
            for e in range(3):
                at = e * tris + (l // per_tile) * LANES
                for i in range(2):
                    for c in range(2):
                        block = acc[i][e * rhs + c * half:e * rhs + (c + 1) * half]
                        p_own[c, i * half:(i + 1) * half, at:at + LANES] = block

    p_send[...] = p_own[1 - core]
    swap = pltpu.make_async_remote_copy(
        src_ref=p_send, dst_ref=p_recv, send_sem=psend_sem, recv_sem=precv_sem,
        device_id=(me, 1 - core), device_id_type=MESH,
    )
    swap.start()
    swap.wait_recv()
    ready = (p_own[core] + p_recv[...]).astype(BF16)

    def fill(g):
        routed = dot(ready, route[...]).astype(BF16)
        for j in range(GROUP):
            send[g * GROUP + j] = routed[:, j * LANES:(j + 1) * LANES]

    if groups == 1:
        fill(0)
    else:
        def fill_step(g, carry):
            build_route(g)
            fill(g)
            return carry

        lax.fori_loop(0, groups, fill_step, 0)

    def block_copy(k):
        to = lax.rem(me + k, peers)
        return pltpu.make_async_remote_copy(
            src_ref=send.at[to], dst_ref=recv.at[me],
            send_sem=send_sem.at[to], recv_sem=recv_sem.at[me],
            device_id=(to, core), device_id_type=MESH,
        )

    def block_arrival(k):
        source = lax.rem(me + k, peers)
        return pltpu.make_async_remote_copy(
            src_ref=send.at[source], dst_ref=recv.at[source],
            send_sem=send_sem.at[source], recv_sem=recv_sem.at[source],
            device_id=(source, core), device_id_type=MESH,
        )

    def start_block(k, carry):
        block_copy(k).start()
        return carry

    lax.fori_loop(1, peers, start_block, 0)
    recv[me] = send[me]

    scatter_ids = jnp.concatenate(
        [
            jnp.full((share, 1), -1, jnp.int32), lower_col,
            jnp.full((LANES - 2 * share, 1), -1, jnp.int32),
            upper_col, jnp.full((LANES - share, 1), -1, jnp.int32),
        ],
        axis=0,
    )
    scatter = bits(iota((2 * LANES, EDGE_DEV), 1) == scatter_ids)

    def take_block(k, carry):
        block_arrival(k).wait_recv()
        return carry

    lax.fori_loop(1, peers, take_block, 0)

    def gathered(g):
        lhs = jnp.concatenate([recv[g * GROUP + j] for j in range(GROUP)], axis=1)
        return lax.dot_general(lhs, collect[...], NT, preferred_element_type=F32)

    if groups == 1:
        edges = gathered(0)
    else:
        def gather_step(g, total):
            build_collect(g)
            return total + gathered(g)

        edges = lax.fori_loop(
            0, groups, gather_step, jnp.zeros((2 * half, EDGE_DEV + LANES), F32)
        )

    rim[...] = edges[:, EDGE_DEV:]
    up = pltpu.make_async_remote_copy(
        src_ref=rim, dst_ref=rim_low, send_sem=rim_send.at[0], recv_sem=rim_recv.at[0],
        device_id=(jnp.minimum(me + 1, peers - 1), core), device_id_type=MESH,
    )
    down = pltpu.make_async_remote_copy(
        src_ref=rim, dst_ref=rim_up, send_sem=rim_send.at[1], recv_sem=rim_recv.at[1],
        device_id=(jnp.maximum(me - 1, 0), core), device_id_type=MESH,
    )
    has_up, has_down = me < peers - 1, me > 0
    pl.when(has_up)(up.start)
    pl.when(has_down)(down.start)
    pl.when(has_down)(up.wait_recv)
    pl.when(has_up)(down.wait_recv)
    hi, lo = split(jnp.concatenate([rim_low[...], rim_up[...]], axis=1))
    total = edges[:, :EDGE_DEV] + dot(hi, scatter) + dot(lo, scatter)
    out_ref[0] = total[:half]
    out_ref[1] = total[half:]

    pl.when(has_up)(up.wait_send)
    pl.when(has_down)(down.wait_send)
    swap.wait_send()

    def sent(k, carry):
        weight_copy(k).wait_send()
        block_copy(k).wait_send()
        return carry

    lax.fori_loop(1, peers, sent, 0)


def body(coefficients, local_to_target, send_map, test_weight, slot_edge, shared_edges):
    peers, cap = send_map.shape[1], send_map.shape[2]
    leaves, cones, comps, rhs, r = coefficients.shape
    points = local_to_target.shape[3]
    share = shared_edges.shape[2]
    capp = max(cap, 16)
    tris = leaves * TRI_LEAF
    half = rhs // 2
    width = GROUP * LANES
    any_spec = pl.BlockSpec(memory_space=pl.ANY)
    vmem_spec = pl.BlockSpec(memory_space=pltpu.VMEM)
    dma = pltpu.SemaphoreType.DMA
    return pl.pallas_call(
        functools.partial(kernel, peers, cap, capp, leaves, rhs, share),
        out_shape=jax.ShapeDtypeStruct((2, half, EDGE_DEV), F32),
        in_specs=[any_spec, any_spec, vmem_spec, any_spec, vmem_spec, vmem_spec],
        out_specs=vmem_spec,
        scratch_shapes=[
            pltpu.VMEM(coefficients.shape, BF16),
            pltpu.VMEM(local_to_target.shape, BF16),
            pltpu.VMEM((leaves, comps * rhs, points), F32),
            pltpu.VMEM((peers, capp, 9 * QUAD) if capp != cap else (1, 16, LANES), BF16),
            pltpu.VMEM((peers, capp, 9 * QUAD), BF16),
            pltpu.VMEM((3 * tris, width), BF16),
            pltpu.VMEM((EDGE_DEV + LANES, width), BF16),
            pltpu.VMEM((peers, LANES), jnp.int32),
            pltpu.VMEM((peers, LANES), jnp.int32),
            pltpu.VMEM((2, 2 * half, 3 * tris), F32),
            pltpu.VMEM((2 * half, 3 * tris), F32),
            pltpu.VMEM((2 * half, 3 * tris), F32),
            pltpu.VMEM((peers, 2 * half, LANES), BF16),
            pltpu.VMEM((peers, 2 * half, LANES), BF16),
            pltpu.VMEM((2 * half, LANES), F32),
            pltpu.VMEM((2 * half, LANES), F32),
            pltpu.VMEM((2 * half, LANES), F32),
            dma, dma((leaves,)), dma, dma, dma((peers,)), dma((peers,)), dma, dma,
            dma((peers,)), dma((peers,)), dma((2,)), dma((2,)),
        ],
        compiler_params=pltpu.CompilerParams(
            collective_id=0, has_side_effects=True, vmem_limit_bytes=48 * 1024 * 1024
        ),
    )(coefficients, local_to_target, send_map, test_weight, slot_edge, shared_edges)


def solution(mesh):
    placed = (
        P("leaf", "cone", None, None, None),
        P("leaf", "cone", None, None),
        P("leaf", None, None),
        P("leaf", None, None, None),
        P(None, "leaf", None, None),
        P("leaf", None, None),
    )
    return jax.shard_map(
        body, mesh=mesh, in_specs=placed, out_specs=P(None, "cone", "leaf"), check_vma=False
    )
```

time: 121 us -> 30.1 us (0.25)
  the two profiles are of different devices: /device:TPU:6 before, /device:TPU:0 now
where the time goes in v1:
time: 30.1 us; the launch traced here: 29.8 us
  Pallas kernels  25 us (83%)
  local copies, waits for them, and re-layouts  4.77 us (16%)
    pallas_call x1, Pallas kernels, body(): pl.pallas_call(functools.partial(kernel, peers, cap, capp, leaves, rhs, s...  25 us
    unnamed x11, local copies, waits for them, and re-layouts  4.77 us

profile of v1, /device:TPU:0, one launch (start us, length us, event | category | flops | bytes accessed | tf_op | source)
XLA Modules:
  0.0 29.8 jit_solution(1942255757918623390)
XLA Ops:
  0.0 0.0 copy-start
  0.0 1.1 %copy-done = bf16[8,2,3,32,256]{4,3,2,1,0:T(8,128)(2,1)S(1)} copy-done((bf16[8,2,3,32,256]{4,3,2,1,0:T(8,128)(2,1)S(1)}, bf16[8,2,3,32,256]{4,3,2,1,0:T(8,128)(2,1)}, u32[]{:S(2)}) %copy-start) | copy-done | bytes 786456
  1.1 0.0 copy-start.1
  1.1 0.9 %copy-done.1 = bf16[1,16,32,108]{3,2,1,0:T(8,128)(2,1)S(1)} copy-done((bf16[1,16,32,108]{3,2,1,0:T(8,128)(2,1)S(1)}, bf16[1,16,32,108]{3,2,1,0:T(8,128)(2,1)}, u32[]{:S(2)}) %copy-start.1) | copy-done | bytes 110616
  2.0 0.0 copy-start.2
  2.0 0.7 %copy-done.2 = s32[3,1,16,32]{3,2,1,0:T(8,128)S(1)} copy-done((s32[3,1,16,32]{3,2,1,0:T(8,128)S(1)}, s32[3,1,16,32]{3,2,1,0:T(8,128)}, u32[]{:S(2)}) %copy-start.2) | copy-done | bytes 6168
  2.8 0.0 copy-start.3
  2.8 0.7 %copy-done.3 = s32[1,16,32]{2,1,0:T(8,128)S(1)} copy-done((s32[1,16,32]{2,1,0:T(8,128)S(1)}, s32[1,16,32]{2,1,0:T(8,128)}, u32[]{:S(2)}) %copy-start.3) | copy-done | bytes 2072
  3.5 0.0 copy-start.4
  3.5 0.7 %copy-done.4 = s32[1,2,32]{2,1,0:T(2,128)S(1)} copy-done((s32[1,2,32]{2,1,0:T(2,128)S(1)}, s32[1,2,32]{2,1,0:T(2,128)}, u32[]{:S(2)}) %copy-start.4) | copy-done | bytes 280
  4.2 25.0 %shard_map.64 = f32[2,16,384]{2,1,0:T(8,128)S(1)} custom-call(bf16[8,2,3,32,256]{4,3,2,1,0:T(8,128)(2,1)S(1)} %copy-done, bf16[8,2,256,768]{3,2,1,0:T(8,128)(2,1)} %op_hbm.1, s32[1,16,32]{2,1,0:T(8,128)S(1)} %copy-done.3, bf16[1,16,32,108]{3,2,1,0:T(8,128)(2,1)S(1)} %copy-done.1, s32[3,1,16,32]{3,2,1,0:T(8,128)S(1)} %copy-done.2, s32[1,2,32]{2,1,0:T(2,128)S(1)} %copy-done.4), custom_call_target="tpu_custom_call" | custom-call | tf_op jit(solution)/shard_map/pallas_call | solution.py:341
  29.2 0.6 %copy.8 = f32[2,16,384]{2,1,0:T(8,128)} copy(f32[2,16,384]{2,1,0:T(8,128)S(1)} %shard_map.64) | data formatting | bytes 98304
Async XLA Ops:
  0.0 1.1 %copy-start = (bf16[8,2,3,32,256]{4,3,2,1,0:T(8,128)(2,1)S(1)}, bf16[8,2,3,32,256]{4,3,2,1,0:T(8,128)(2,1)}, u32[]{:S(2)}) copy-start(bf16[8,2,3,32,256]{4,3,2,1,0:T(8,128)(2,1)} %coef_hbm.1) | copy-start | bytes 2359300
  1.1 0.9 %copy-start.1 = (bf16[1,16,32,108]{3,2,1,0:T(8,128)(2,1)S(1)}, bf16[1,16,32,108]{3,2,1,0:T(8,128)(2,1)}, u32[]{:S(2)}) copy-start(bf16[1,16,32,108]{3,2,1,0:T(8,128)(2,1)} %weight_hbm.1) | copy-start | bytes 331780
  2.0 0.7 %copy-start.2 = (s32[3,1,16,32]{3,2,1,0:T(8,128)S(1)}, s32[3,1,16,32]{3,2,1,0:T(8,128)}, u32[]{:S(2)}) copy-start(s32[3,1,16,32]{3,2,1,0:T(8,128)} %edge_ref.1) | copy-start | bytes 18436
  2.8 0.7 %copy-start.3 = (s32[1,16,32]{2,1,0:T(8,128)S(1)}, s32[1,16,32]{2,1,0:T(8,128)}, u32[]{:S(2)}) copy-start(s32[1,16,32]{2,1,0:T(8,128)} %map_ref.1) | copy-start | bytes 6148
  3.5 0.7 %copy-start.4 = (s32[1,2,32]{2,1,0:T(2,128)S(1)}, s32[1,2,32]{2,1,0:T(2,128)}, u32[]{:S(2)}) copy-start(s32[1,2,32]{2,1,0:T(2,128)} %shared_ref.1) | copy-start | bytes 772

commit v2 on v1

--- a/solution.py
+++ b/solution.py
@@ -44,11 +44,11 @@
 
 def kernel(
     peers, cap, capp, leaves, rhs, share,
-    coef_hbm, op_hbm, map_ref, weight_hbm, edge_ref, shared_ref,
+    coef_hbm, op_hbm, map_hbm, weight_hbm, edge_hbm, shared_hbm,
     out_ref,
-    coef, op, field, wpad, wbuf, route, collect, sel_x, col_x, p_own, p_send, p_recv,
+    map_ref, edge_ref, shared_ref, coef, op, field, wpad, wbuf, route, collect, sel_x, col_x, p_own, p_send, p_recv,
     send, recv, rim, rim_low, rim_up,
-    coef_sem, op_sem, wpad_sem, wown_sem, wsend_sem, wrecv_sem, psend_sem, precv_sem,
+    map_sem, edge_sem, shared_sem, coef_sem, op_sem, wpad_sem, wown_sem, wsend_sem, wrecv_sem, psend_sem, precv_sem,
     send_sem, recv_sem, rim_send, rim_recv,
 ):
     me = lax.axis_index("leaf")
@@ -56,11 +56,17 @@
     points = 2 * QUAD * TRI_LEAF
     tris = leaves * TRI_LEAF
     half = rhs // 2
-    width = GROUP * LANES
     groups = peers // GROUP
 
     coef_copy = pltpu.make_async_copy(coef_hbm, coef, coef_sem)
     coef_copy.start()
+    small = [
+        pltpu.make_async_copy(map_hbm, map_ref, map_sem),
+        pltpu.make_async_copy(edge_hbm, edge_ref, edge_sem),
+        pltpu.make_async_copy(shared_hbm, shared_ref, shared_sem),
+    ]
+    for copy in small:
+        copy.start()
     op_copies = []
     for l in range(leaves):
         copy = pltpu.make_async_copy(op_hbm.at[l], op.at[l], op_sem.at[l])
@@ -91,88 +97,10 @@
     own_weights = pltpu.make_async_copy(weight_src.at[me], wbuf.at[me], wown_sem)
     own_weights.start()
 
-    pl.semaphore_wait(barrier, peers)
-
-    def weight_copy(k):
-        to = lax.rem(me + k, peers)
-        return pltpu.make_async_remote_copy(
-            src_ref=weight_src.at[to], dst_ref=wbuf.at[me],
-            send_sem=wsend_sem.at[to], recv_sem=wrecv_sem.at[me],
-            device_id=(to, core), device_id_type=MESH,
-        )
-
-    def weight_arrival(k):
-        source = lax.rem(me + k, peers)
-        return pltpu.make_async_remote_copy(
-            src_ref=weight_src.at[source], dst_ref=wbuf.at[source],
-            send_sem=wsend_sem.at[source], recv_sem=wrecv_sem.at[source],
-            device_id=(source, core), device_id_type=MESH,
-        )
-
-    def start_weight(k, carry):
-        weight_copy(k).start()
-        return carry
-
-    lax.fori_loop(1, peers, start_weight, 0)
-
-    maps = map_ref[0]
-    filler = jnp.full((peers, LANES - 3 * cap), -1, jnp.int32)
-    sel_x[...] = jnp.concatenate([maps, maps, maps, filler], axis=1)
-    col_x[...] = jnp.concatenate([edge_ref[0, 0], edge_ref[1, 0], edge_ref[2, 0], filler], axis=1)
-    lower_col = column(shared_ref[0, 0:1, :])
-    upper_col = column(shared_ref[0, 1:2, :])
-    rim_cols = jnp.concatenate(
-        [lower_col, upper_col, jnp.full((LANES - 2 * share, 1), -2, jnp.int32)], axis=0
-    )
-    lane_e = iota((1, LANES), 1)
-
-    def build_route(g):
-        for j in range(GROUP):
-            row = sel_x[pl.ds(g * GROUP + j, 1), :]
-            for e in range(3):
-                ours = jnp.logical_and(lane_e >= e * cap, lane_e < (e + 1) * cap)
-                key = jnp.where(ours, row, -1)
-                route[e * tris:(e + 1) * tris, j * LANES:(j + 1) * LANES] = bits(
-                    iota((tris, LANES), 0) == key
-                )
-
-    def build_collect(g):
-        for j in range(GROUP):
-            row = col_x[pl.ds(g * GROUP + j, 1), :]
-            lanes = slice(j * LANES, (j + 1) * LANES)
-            collect[:EDGE_DEV, lanes] = bits(iota((EDGE_DEV, LANES), 0) == row)
-            collect[EDGE_DEV:, lanes] = bits(rim_cols == row)
-
-    if groups == 1:
-        build_route(0)
-        build_collect(0)
-
-    coef_copy.wait()
-    for l in range(leaves):
-        op_copies[l].wait()
-        total = None
-        for k in range(coef.shape[1]):
-            term = dot(coef[l, k].reshape(3 * rhs, -1), op[l, k])
-            total = term if total is None else total + term
-        field[l] = total
-
-    own_weights.wait()
-
-    def take_weight(k, carry):
-        weight_arrival(k).wait_recv()
-        return carry
-
-    lax.fori_loop(1, peers, take_weight, 0)
-    if capp != cap:
-        maps = jnp.concatenate([maps, jnp.full((peers, capp - cap), -1, jnp.int32)], axis=1)
-    slots = jnp.concatenate([maps[d:d + 1] for d in range(peers)], axis=1)
-    pick = bits(iota((tris, peers * capp), 0) == slots)
-    by_tri = dot(pick, wbuf[...].reshape(peers * capp, -1)).astype(BF16)
     rows = iota((16 * QUAD, 9 * QUAD), 0)
     point, pair = rows >> 4, rows & 15
     e_of = (pair * 11) >> 5
-    order = (pair < 9) & (iota(rows.shape, 1) == e_of * (3 * QUAD) + point * 3 + pair - 3 * e_of)
-    turned = lax.dot_general(bits(order), by_tri, NT, preferred_element_type=F32).astype(BF16)
+    order = bits((pair < 9) & (iota(rows.shape, 1) == e_of * (3 * QUAD) + point * 3 + pair - 3 * e_of))
     tri_row = (iota((tris, points), 0) & (TRI_LEAF - 1)) * (2 * QUAD)
     lane_q = iota((tris, points), 1)
     spread = bits((lane_q >= tri_row) & (lane_q < tri_row + 2 * QUAD))
@@ -187,9 +115,89 @@
     tri_lane = iota((1, tris), 1)
     lane_group = iota((1, LANES), 1) // TRI_LEAF
 
+    small[0].wait()
+    maps = map_ref[0]
+    filler = jnp.full((peers, LANES - 3 * cap), -1, jnp.int32)
+    sel_x[...] = jnp.concatenate([maps, maps, maps, filler], axis=1)
+    if capp != cap:
+        maps = jnp.concatenate([maps, jnp.full((peers, capp - cap), -1, jnp.int32)], axis=1)
+    slots = jnp.concatenate([maps[d:d + 1] for d in range(peers)], axis=1)
+    pick = bits(iota((tris, peers * capp), 0) == slots)
+    small[1].wait()
+    small[2].wait()
+    col_x[...] = jnp.concatenate([edge_ref[0, 0], edge_ref[1, 0], edge_ref[2, 0], filler], axis=1)
+    lower_col = column(shared_ref[0, 0:1, :])
+    upper_col = column(shared_ref[0, 1:2, :])
+    rim_cols = jnp.concatenate(
+        [lower_col, upper_col, jnp.full((LANES - 2 * share, 1), -2, jnp.int32)], axis=0
+    )
+    lane_e = iota((1, LANES), 1)
     per_tile = LANES // TRI_LEAF
     tiles = tris // LANES
+
+    def build_route(g):
+        for j in range(GROUP):
+            row = sel_x[pl.ds(g * GROUP + j, 1), :]
+            for e in range(3):
+                ours = jnp.logical_and(lane_e >= e * cap, lane_e < (e + 1) * cap)
+                key = jnp.where(ours, row, -1)
+                for t in range(tiles):
+                    at = (t * 3 + e) * LANES
+                    route[at:at + LANES, j * LANES:(j + 1) * LANES] = bits(
+                        iota((LANES, LANES), 0) + t * LANES == key
+                    )
+
+    def build_collect(g):
+        for j in range(GROUP):
+            row = col_x[pl.ds(g * GROUP + j, 1), :]
+            lanes = slice(j * LANES, (j + 1) * LANES)
+            collect[:EDGE_DEV, lanes] = bits(iota((EDGE_DEV, LANES), 0) == row)
+            collect[EDGE_DEV:, lanes] = bits(rim_cols == row)
+
+    pl.semaphore_wait(barrier, peers)
+
+    def weight_copy(k):
+        to = lax.rem(me + k, peers)
+        return pltpu.make_async_remote_copy(
+            src_ref=weight_src.at[to], dst_ref=wbuf.at[me],
+            send_sem=wsend_sem.at[to], recv_sem=wrecv_sem.at[me],
+            device_id=(to, core), device_id_type=MESH,
+        )
+
+    def weight_arrival(k):
+        source = lax.rem(me + k, peers)
+        return pltpu.make_async_remote_copy(
+            src_ref=weight_src.at[source], dst_ref=wbuf.at[source],
+            send_sem=wsend_sem.at[source], recv_sem=wrecv_sem.at[source],
+            device_id=(source, core), device_id_type=MESH,
+        )
+
+    def start_weight(k, carry):
+        weight_copy(k).start()
+        return carry
+
+    lax.fori_loop(1, peers, start_weight, 0)
+
+    coef_copy.wait()
+    for l in range(leaves):
+        op_copies[l].wait()
+        total = None
+        for k in range(coef.shape[1]):
+            term = dot(coef[l, k].reshape(3 * rhs, -1), op[l, k])
+            total = term if total is None else total + term
+        field[l] = total
+
+    own_weights.wait()
+
+    def take_weight(k, carry):
+        weight_arrival(k).wait_recv()
+        return carry
+
+    lax.fori_loop(1, peers, take_weight, 0)
+    by_tri = dot(pick, wbuf[...].reshape(peers * capp, -1)).astype(BF16)
+    turned = lax.dot_general(order, by_tri, NT, preferred_element_type=F32).astype(BF16)
     acc = None
+    swaps = []
     for l in range(leaves):
         mine = jnp.where((tri_lane >= l * TRI_LEAF) & (tri_lane < (l + 1) * TRI_LEAF), turned, 0)
         wide = dot(mine, spread)
@@ -210,21 +218,29 @@
         parts = [summed[:, :LANES] * keep, summed[:, LANES:] * keep]
         acc = parts if l % per_tile == 0 else [a + b for a, b in zip(acc, parts)]
         if l % per_tile == per_tile - 1:
+            tile = l // per_tile
             for e in range(3):
-                at = e * tris + (l // per_tile) * LANES
                 for i in range(2):
                     for c in range(2):
                         block = acc[i][e * rhs + c * half:e * rhs + (c + 1) * half]
-                        p_own[c, i * half:(i + 1) * half, at:at + LANES] = block
-
-    p_send[...] = p_own[1 - core]
-    swap = pltpu.make_async_remote_copy(
-        src_ref=p_send, dst_ref=p_recv, send_sem=psend_sem, recv_sem=precv_sem,
-        device_id=(me, 1 - core), device_id_type=MESH,
-    )
-    swap.start()
-    swap.wait_recv()
-    ready = (p_own[core] + p_recv[...]).astype(BF16)
+                        p_own[c, tile, i * half:(i + 1) * half, e * LANES:(e + 1) * LANES] = block
+
+            p_send[tile] = p_own[1 - core, tile]
+            swap = pltpu.make_async_remote_copy(
+                src_ref=p_send.at[tile], dst_ref=p_recv.at[tile],
+                send_sem=psend_sem.at[tile], recv_sem=precv_sem.at[tile],
+                device_id=(me, 1 - core), device_id_type=MESH,
+            )
+            swap.start()
+            swaps.append(swap)
+
+    if groups == 1:
+        build_route(0)
+    sums = []
+    for tile in range(tiles):
+        swaps[tile].wait_recv()
+        sums.append((p_own[core, tile] + p_recv[tile]).astype(BF16))
+    ready = jnp.concatenate(sums, axis=1)
 
     def fill(g):
         routed = dot(ready, route[...]).astype(BF16)
@@ -263,6 +279,8 @@
 
     lax.fori_loop(1, peers, start_block, 0)
     recv[me] = send[me]
+    if groups == 1:
+        build_collect(0)
 
     scatter_ids = jnp.concatenate(
         [
@@ -316,7 +334,8 @@
 
     pl.when(has_up)(up.wait_send)
     pl.when(has_down)(down.wait_send)
-    swap.wait_send()
+    for swap in swaps:
+        swap.wait_send()
 
     def sent(k, carry):
         weight_copy(k).wait_send()
@@ -341,9 +360,12 @@
     return pl.pallas_call(
         functools.partial(kernel, peers, cap, capp, leaves, rhs, share),
         out_shape=jax.ShapeDtypeStruct((2, half, EDGE_DEV), F32),
-        in_specs=[any_spec, any_spec, vmem_spec, any_spec, vmem_spec, vmem_spec],
+        in_specs=[any_spec] * 6,
         out_specs=vmem_spec,
         scratch_shapes=[
+            pltpu.VMEM(send_map.shape, jnp.int32),
+            pltpu.VMEM(slot_edge.shape, jnp.int32),
+            pltpu.VMEM(shared_edges.shape, jnp.int32),
             pltpu.VMEM(coefficients.shape, BF16),
             pltpu.VMEM(local_to_target.shape, BF16),
             pltpu.VMEM((leaves, comps * rhs, points), F32),
@@ -353,19 +375,20 @@
             pltpu.VMEM((EDGE_DEV + LANES, width), BF16),
             pltpu.VMEM((peers, LANES), jnp.int32),
             pltpu.VMEM((peers, LANES), jnp.int32),
-            pltpu.VMEM((2, 2 * half, 3 * tris), F32),
-            pltpu.VMEM((2 * half, 3 * tris), F32),
-            pltpu.VMEM((2 * half, 3 * tris), F32),
+            pltpu.VMEM((2, tris // LANES, 2 * half, 3 * LANES), F32),
+            pltpu.VMEM((tris // LANES, 2 * half, 3 * LANES), F32),
+            pltpu.VMEM((tris // LANES, 2 * half, 3 * LANES), F32),
             pltpu.VMEM((peers, 2 * half, LANES), BF16),
             pltpu.VMEM((peers, 2 * half, LANES), BF16),
             pltpu.VMEM((2 * half, LANES), F32),
             pltpu.VMEM((2 * half, LANES), F32),
             pltpu.VMEM((2 * half, LANES), F32),
-            dma, dma((leaves,)), dma, dma, dma((peers,)), dma((peers,)), dma, dma,
+            dma, dma, dma, dma, dma((leaves,)), dma, dma, dma((peers,)), dma((peers,)),
+            dma((tris // LANES,)), dma((tris // LANES,)),
             dma((peers,)), dma((peers,)), dma((2,)), dma((2,)),
         ],
         compiler_params=pltpu.CompilerParams(
-            collective_id=0, has_side_effects=True, vmem_limit_bytes=48 * 1024 * 1024
+            collective_id=0, has_side_effects=True, vmem_limit_bytes=60 * 1024 * 1024
         ),
     )(coefficients, local_to_target, send_map, test_weight, slot_edge, shared_edges)
 

time: 30.1 us -> 28.3 us (0.940)
  local copies, waits for them, and re-layouts: 4.77 us -> 1.42 us
  Pallas kernels: 25 us -> 26.7 us
    unnamed x11 -> x1, local copies, waits for them, and re-layouts: 4.77 us -> 1.42 us
    pallas_call x1, Pallas kernels: 25 us -> 26.7 us  [body(): pl.pallas_call(functools.partial(kernel, peers, cap, capp, leaves, rhs, s...]
where the time goes in v2:
time: 28.3 us; the launch traced here: 28.1 us
  Pallas kernels  26.7 us (94%)
  local copies, waits for them, and re-layouts  1.42 us (5%)
    pallas_call x1, Pallas kernels, body(): pl.pallas_call(functools.partial(kernel, peers, cap, capp, leaves, rhs, s...  26.7 us
    unnamed x1, local copies, waits for them, and re-layouts  1.42 us

profile of v2, /device:TPU:0, one launch (start us, length us, event | category | flops | bytes accessed | tf_op | source)
XLA Modules:
  0.0 28.1 jit_solution(17907162583152071055)
XLA Ops:
  0.0 26.7 %shard_map.64 = f32[2,16,384]{2,1,0:T(8,128)} custom-call(bf16[8,2,3,32,256]{4,3,2,1,0:T(8,128)(2,1)} %coef_hbm.1, bf16[8,2,256,768]{3,2,1,0:T(8,128)(2,1)} %op_hbm.1, s32[1,16,32]{2,1,0:T(8,128)} %map_hbm.1, bf16[1,16,32,108]{3,2,1,0:T(8,128)(2,1)} %weight_hbm.1, s32[3,1,16,32]{3,2,1,0:T(8,128)} %edge_hbm.1, s32[1,2,32]{2,1,0:T(2,128)} %shared_hbm.1), custom_call_target="tpu_custom_call" | custom-call | tf_op jit(solution)/shard_map/pallas_call | solution.py:360
  26.7 1.4 %copy.8 = f32[2,16,384]{2,1,0:T(8,128)} copy(f32[2,16,384]{2,1,0:T(8,128)} %shard_map.64) | data formatting | bytes 98304
